TPU v7x, 128 devices: a whole 4x4x4 slice. The times are simulated.
128 devices in a mesh: visit: 4 (over y), ccd: 32 (over x, z, core).
Axes of the slice: x: 4, y: 4, z: 4, core: 2. Of those that a mesh axis runs over, the one named last changes fastest.
Arguments:
- exposure: bfloat16 [4, 2048, 4096], P('visit', 'ccd'), may hold values from -6 to 6
- offsets: int32 [4, 32, 2], P('visit', 'ccd'), may hold values from -32 to 32
- fraction: float32 [4, 32, 2], P('visit', 'ccd'), may hold values from 0 to 1
- route_patch: int32 [4, 2048], P('visit', 'ccd'), may hold values from 0 to 127, as said below
- route_slot: int32 [4, 2048], P('visit', 'ccd'), may hold values from 0 to 63
- block_weight: bfloat16 [4, 2048], P('visit', 'ccd'), may hold values from 0.25 to 4
- kernel_rows: float32 [33], replicated, may hold values from -1 to 1
- kernel_columns: float32 [33], replicated, may hold values from -1 to 1
Outputs:
- coadded: bfloat16 [512, 65536], P('visit', 'ccd')
- matched: float32 [512, 65536], P('visit', 'ccd')
Inputs may be any that keep to these rules, and one draw needn't show every extreme that they name: `route_patch`: no patch is named by more than 2 of one exposure's 64 blocks; one patch, drawn from the seed, is named by exactly 2 blocks of every exposure.
All inputs are finite; a program needn't handle non-finite values.
Results may differ from a plain program's by a relative error of at most 0.0082.
Values may be sent and summed in bfloat16 or wider, within the bound.
A program may use at most 64 MiB of HBM per device.

v0:
```python
import jax
import jax.numpy as jnp
from jax import lax
from jax.sharding import PartitionSpec as P

BLOCK_ROWS = 32
BLOCK_COLS = 128
MARGIN = 40
HALF_KERNEL = 16


def extended_2(x, sides, width):
    for axis, dim in sides:
        devices, length = (lax.axis_size(axis), x.shape[dim])
        up = [(i, (i + 1) % devices) for i in range(devices - 1)]
        down = [(j, i) for i, j in up]
        last = lax.slice_in_dim(x, length - width, length, axis=dim)
        first = lax.slice_in_dim(x, 0, width, axis=dim)
        before = lax.ppermute(last, axis, up)
        after = lax.ppermute(first, axis, down)
        x = jnp.concatenate([before, x, after], axis=dim)
    return x


def sent_together(arrays, axis, split_dim, concat_dim, along):
    ends, at = ([], 0)
    for a in arrays[:-1]:
        at += a.shape[along]
        ends.append(at)
    both = jnp.concatenate(arrays, axis=along)
    return tuple(
        jnp.split(
            lax.all_to_all(both, axis, split_axis=split_dim, concat_axis=concat_dim, tiled=True),
            ends,
            axis=along,
        )
    )


def lanczos_weights(fraction_part):
    distance = jnp.arange(3, -3, -1).astype(jnp.float32) - fraction_part
    kernel = jnp.sinc(distance) * jnp.sinc(distance / 3.0)
    return (kernel / jnp.sum(kernel)).astype(jnp.bfloat16)


def band_matrix(out_count, in_count, first_lag, weights):
    lag_index = jnp.arange(in_count)[None, :] - jnp.arange(out_count)[:, None] - first_lag
    matrix = jnp.zeros((out_count, in_count), jnp.bfloat16)
    for position in range(weights.shape[0]):
        matrix = jnp.where(lag_index == position, weights[position], matrix)
    return matrix


def column_pass(pixels, window_matrix, rim_width):
    tile_rows = pixels.shape[0]
    widened = jnp.pad(pixels, ((0, 0), (128 - rim_width, 128 - rim_width)))
    block_count = widened.shape[1] // 128 - 2
    blocked = widened.reshape(tile_rows, block_count + 2, 128)
    summed = jnp.zeros((tile_rows, block_count, 128), jnp.float32)
    for part_index in range(3):
        summed = summed + jnp.einsum(
            "rjb,bo->rjo",
            blocked[:, part_index : part_index + block_count],
            window_matrix[128 * part_index : 128 * (part_index + 1)],
            preferred_element_type=jnp.float32,
        )
    return summed.reshape(tile_rows, block_count * 128)


def on_device(
    exposure, offsets, fraction, route_patch, route_slot, block_weight, kernel_rows, kernel_columns
):
    pixel_tile = exposure[0]
    tile_rows, tile_columns = pixel_tile.shape
    extended = extended_2(pixel_tile, (("ccd", 0),), MARGIN)
    row_weights = lanczos_weights(fraction[0, 0, 0])
    column_weights = lanczos_weights(fraction[0, 0, 1])
    row_matrix = band_matrix(
        tile_rows, tile_rows + 2 * MARGIN, MARGIN - offsets[0, 0, 0] - 3, row_weights
    )
    row_warped = jnp.dot(row_matrix, extended, preferred_element_type=jnp.float32).astype(
        jnp.bfloat16
    )
    column_matrix = band_matrix(128, 384, 125 - offsets[0, 0, 1], column_weights).T
    warped = column_pass(row_warped, column_matrix, 0).astype(jnp.bfloat16)
    blocks = warped.reshape(
        tile_rows // BLOCK_ROWS, BLOCK_ROWS, tile_columns // BLOCK_COLS, BLOCK_COLS
    )
    blocks = blocks.transpose(0, 2, 1, 3).reshape(-1, BLOCK_ROWS * BLOCK_COLS)
    block_count = blocks.shape[0]
    visit_count = lax.axis_size("visit")
    owner_count = visit_count * lax.axis_size("ccd")
    capacity = 4 * block_count // owner_count
    destination = route_patch[0]
    block_order = jnp.arange(block_count)
    same_before = (destination[None, :] == destination[:, None]) & (
        block_order[None, :] < block_order[:, None]
    )
    block_rank = jnp.sum(same_before.astype(jnp.int32), axis=1)
    position = destination * capacity + block_rank
    placement = (jnp.arange(owner_count * capacity)[:, None] == position[None, :]).astype(
        jnp.bfloat16
    )
    slot_table = jnp.where(
        route_slot[0][:, None] == jnp.arange(block_count)[None, :],
        block_weight[0][:, None],
        jnp.zeros((), jnp.bfloat16),
    )
    send_pixels = jnp.dot(placement, blocks, preferred_element_type=jnp.float32).astype(
        jnp.bfloat16
    )
    send_weights = jnp.dot(placement, slot_table, preferred_element_type=jnp.float32).astype(
        jnp.bfloat16
    )
    got_pixels, got_weights = sent_together(
        (
            send_pixels.reshape(owner_count, capacity, BLOCK_ROWS * BLOCK_COLS),
            send_weights.reshape(owner_count, capacity, block_count),
        ),
        ("visit", "ccd"),
        0,
        0,
        2,
    )
    got_pixels = got_pixels.reshape(-1, BLOCK_ROWS * BLOCK_COLS)
    got_weights = got_weights.reshape(-1, block_count)
    numerator = lax.dot_general(
        got_weights, got_pixels, (((0,), (0,)), ((), ())), preferred_element_type=jnp.float32
    )
    weight_total = jnp.sum(got_weights.astype(jnp.float32), axis=0)
    slot_values = (numerator / jnp.maximum(weight_total, 1.0)[:, None]).astype(jnp.bfloat16)
    patch_rows = 2 * tile_rows
    patch_columns = tile_columns // 2
    coadded = slot_values.reshape(
        patch_rows // BLOCK_ROWS, patch_columns // BLOCK_COLS, BLOCK_ROWS, BLOCK_COLS
    )
    coadded = coadded.transpose(0, 2, 1, 3).reshape(patch_rows, patch_columns)
    row_kernel = kernel_rows.astype(jnp.bfloat16)
    column_kernel = kernel_columns.astype(jnp.bfloat16)
    row_filter = band_matrix(patch_rows, patch_rows + 2 * HALF_KERNEL, 0, row_kernel)
    column_filter = band_matrix(128, 384, 128 - HALF_KERNEL, column_kernel).T
    framed = extended_2(coadded, (("visit", 0), ("ccd", 1)), HALF_KERNEL)
    smoothed = jnp.dot(row_filter, framed, preferred_element_type=jnp.float32).astype(jnp.bfloat16)
    matched = column_pass(smoothed, column_filter, HALF_KERNEL)
    return (coadded, matched)


def solution(mesh):
    placed = (
        P("visit", "ccd", None),
        P("visit", "ccd", None),
        P("visit", "ccd", None),
        P("visit", "ccd"),
        P("visit", "ccd"),
        P("visit", "ccd"),
        P(),
        P(),
    )
    return jax.shard_map(
        on_device,
        mesh=mesh,
        in_specs=placed,
        out_specs=(P("visit", "ccd"), P("visit", "ccd")),
        check_vma=False,
    )
```

profile of v0, /device:TPU:97, one launch (start us, length us, event | category | flops | bytes accessed | tf_op | source)
XLA Modules:
  0.0 130.0 jit_solution(111050077930407504)
XLA Ops:
  0.6 1.1 slice_bitcast_fusion.1
  1.8 2.3 %collective-permute-start = (bf16[40,4096]{1,0:T(8,128)(2,1)S(1)}, bf16[40,4096]{1,0:T(8,128)(2,1)S(1)}, u32[]{:S(2)}, u32[]{:S(2)}) collective-permute-start(bf16[40,4096]{1,0:T(8,128)(2,1)S(1)} %get-tuple-element.15), channel_id=1, source_target_pairs={{0,1},{1,2},{2,3},{3,4},{4,5},{5,6},{6,7},{7,8},{8,9},{9,10},{10,1... | collective-permute-start | bytes 983048 | tf_op jit(solution)/shard_map/ppermute | solution.py:19
  4.1 2.2 %collective-permute-start.1 = (bf16[40,4096]{1,0:T(8,128)(2,1)S(1)}, bf16[40,4096]{1,0:T(8,128)(2,1)S(1)}, u32[]{:S(2)}, u32[]{:S(2)}) collective-permute-start(bf16[40,4096]{1,0:T(8,128)(2,1)S(1)} %get-tuple-element.16), channel_id=1, source_target_pairs={{1,0},{2,1},{3,2},{4,3},{5,4},{6,5},{7,6},{8,7},{9,8},{10,9},{11,1... | collective-permute-start | bytes 983048 | tf_op jit(solution)/shard_map/ppermute | solution.py:20
  6.3 1.3 %fusion.339 = (f32[1,1,1]{2,1,0:T(1,128)}, f32[1,1,1]{2,1,0:T(1,128)}) fusion(f32[1,1,2]{2,1,0:T(1,128)} %param.11), kind=kLoop, calls=%fused_computation.406 | loop fusion | bytes 16 | tf_op jit(solution)/shard_map/slice | solution.py:77
  7.6 1.3 fusion.288
  8.9 1.3 %divide_convert_fusion.1 = bf16[6]{0:T(256)(128)(2,1)S(1)} fusion(f32[]{:T(128)} %fusion.288, f32[]{:T(128)} %bitcast.4), kind=kLoop, calls=%fused_computation.351 | loop fusion | flops 444 | bytes 20 | tf_op jit(solution)/shard_map/convert_element_type | solution.py:43
  10.2 0.7 fusion.341
  10.9 1.3 %fusion.340 = (s32[1,1,1]{2,1,0:T(1,128)}, s32[1,1,1]{2,1,0:T(1,128)}) fusion(s32[1,1,2]{2,1,0:T(1,128)} %param.10), kind=kLoop, calls=%fused_computation.407 | loop fusion | bytes 16 | tf_op jit(solution)/shard_map/slice | solution.py:84
  12.2 1.2 fusion.287
  13.4 0.9 convert_reduce_fusion.1
  14.3 0.7 fusion.274
  15.0 0.9 convolution_convert_fusion.3
  15.9 0.1 copy.47
  17.3 1.2 divide_convert_fusion
  18.6 0.7 fusion.338
  19.2 3.8 %fusion.59 = bf16[384,128]{1,0:T(8,128)(2,1)S(1)} fusion(s32[]{:T(128)} %bitcast.14, bf16[]{:T(256)} %bitcast.21, bf16[]{:T(256)} %bitcast.20, bf16[]{:T(256)} %bitcast.19, bf16[]{:T(256)} %bitcast.18, bf16[]{:T(256)} %bitcast.17, bf16[]{:T(256)} %bitcast.16), kind=kLoop, calls=%fused_computation.72 | loop fusion | flops 688128 | bytes 98320 | tf_op jit(solution)/shard_map/jit(_where)/select_n | solution.py:50
  23.1 0.0 collective-permute-done
  23.1 0.0 collective-permute-done.1
  23.1 5.1 %convolution_convert_fusion.1 = bf16[64,4096]{1,0:T(8,128)(2,1)S(1)} fusion(bf16[40,4096]{1,0:T(8,128)(2,1)S(1)} %collective-permute-done.1, bf16[64,4096]{1,0:T(8,128)(2,1)} %bitcast.161, bf16[40,4096]{1,0:T(8,128)(2,1)S(1)} %collective-permute-done, s32[]{:T(128)} %bitcast.3, bf16[]{:T(256)} %bitcast.10, bf16[]{:T(256)} %bitcast.9, bf16[]{:T(256)} %bitcast.8, ...), kind=kOutput, calls=%fused_computation.2 | convolution fusion | flops 79427584 | bytes 1703952 | tf_op jit(solution)/shard_map/dot_general | solution.py:81
  28.2 0.3 reshape.47
  28.5 0.3 fusion.16
  28.8 0.3 convolution_add_fusion.3
  29.1 0.3 fusion.3
  29.4 0.2 copy.46
  29.6 0.7 convolution_convert_fusion
  30.3 2.6 %reshape.49 = bf16[128,2,4096]{2,1,0:T(2,128)(2,1)} reshape(bf16[256,4096]{1,0:T(8,128)(2,1)S(1)} %convolution_convert_fusion) | data formatting | bytes 4194304 | tf_op jit(solution)/shard_map/reshape | solution.py:117
  33.0 5.2 %pad_maximum_fusion = bf16[128,2,4160]{2,1,0:T(2,128)(2,1)} fusion(bf16[128,2,64]{2,1,0:T(2,128)(2,1)S(1)} %bitcast.164, bf16[128,2,4096]{2,1,0:T(2,128)(2,1)} %reshape.49), kind=kLoop, calls=%fused_computation.6 | loop fusion | flops 4259840 | bytes 4259840 | tf_op jit(solution)/shard_map/concatenate | solution.py:30
  38.1 0.0 copy-start.1
  38.1 0.0 copy-start.2
  38.1 11.2 %all-to-all-start = ((bf16[128,2,4160]{2,1,0:T(2,128)(2,1)}), bf16[128,2,4160]{2,1,0:T(2,128)(2,1)S(1)}, u32[]{:S(2)}, u32[]{:S(2)}) async-start(bf16[128,2,4160]{2,1,0:T(2,128)(2,1)} %pad_maximum_fusion), calls=%async_computation | async-start | bytes 4325376 | tf_op jit(solution)/shard_map/all_to_all | solution.py:33
  49.4 0.0 copy-done.1
  49.4 0.0 copy-done.2
  49.4 0.7 fusion.334
  50.1 0.7 fusion.335
  50.9 20.9 %fusion.65 = bf16[384,128]{1,0:T(8,128)(2,1)S(1)} fusion(bf16[]{:T(256)} %bitcast.98, bf16[]{:T(256)} %bitcast.97, bf16[]{:T(256)} %bitcast.96, bf16[]{:T(256)} %bitcast.95, bf16[]{:T(256)} %bitcast.94, bf16[]{:T(256)} %bitcast.93, bf16[]{:T(256)} %bitcast.92, bf16[]{:T(256)} %bitcast.91, bf16[]{:T(256)} %bitcast.90, bf16[]{:T(256)} %bitcast.89, ...), kind=kLoop, calls=%fused_computation.78 | loop fusion | flops 3342336 | bytes 98370 | tf_op jit(solution)/shard_map/jit(_where)/select_n | solution.py:50
  71.8 4.9 %all-to-all-done = bf16[128,2,4160]{2,1,0:T(2,128)(2,1)S(1)} async-done(((bf16[128,2,4160]{2,1,0:T(2,128)(2,1)}), bf16[128,2,4160]{2,1,0:T(2,128)(2,1)S(1)}, u32[]{:S(2)}, u32[]{:S(2)}) %all-to-all-start) | async-done | bytes 2129952 | tf_op jit(solution)/shard_map/all_to_all | solution.py:33
  76.7 0.1 copy.64
  76.8 0.1 convert_reduce_fusion
  77.0 2.4 %split.9 = bf16[128,2,4096]{2,1,0:T(2,128)(2,1)S(1)} slice(bf16[128,2,4160]{2,1,0:T(2,128)(2,1)S(1)} %all-to-all-done), slice={[0:128], [0:2], [0:4096]} | slice | bytes 4194304 | tf_op jit(solution)/shard_map/split | solution.py:32
  79.3 2.4 %fusion.4 = bf16[8,8,32,128]{3,1,2,0:T(8,128)(2,1)S(1)} fusion(bf16[128,2,64]{0,2,1:T(8,128)(2,1)S(1)} %copy.64, bf16[128,2,4096]{2,1,0:T(2,128)(2,1)S(1)} %split.9, f32[64]{0:T(128)S(1)} %broadcast_maximum_fusion), kind=kOutput, calls=%fused_computation.13 | convolution fusion | flops 134742016 | bytes 2654464 | tf_op jit(solution)/shard_map/dot_general | solution.py:127
  81.8 0.1 copy.70
  81.9 0.2 copy.50
  82.1 0.1 copy.83
  82.3 0.0 copy-start
  82.3 2.3 %collective-permute-start.2 = (bf16[16,2048]{1,0:T(8,128)(2,1)S(1)}, bf16[16,2048]{1,0:T(8,128)(2,1)S(1)}, u32[]{:S(2)}, u32[]{:S(2)}) collective-permute-start(bf16[16,2048]{1,0:T(8,128)(2,1)S(1)} %get-tuple-element.14), channel_id=1, source_target_pairs={{0,32},{32,64},{64,96},{1,33},{33,65},{65,97},{2,34},{34,66},{66,9... | collective-permute-start | bytes 196616 | tf_op jit(solution)/shard_map/ppermute | solution.py:19
  84.6 0.7 fusion.336
  85.3 1.5 %collective-permute-start.3 = (bf16[16,2048]{1,0:T(8,128)(2,1)S(1)}, bf16[16,2048]{1,0:T(8,128)(2,1)S(1)}, u32[]{:S(2)}, u32[]{:S(2)}) collective-permute-start(bf16[16,2048]{1,0:T(8,128)(2,1)S(1)} %get-tuple-element.13), channel_id=1, source_target_pairs={{32,0},{64,32},{96,64},{33,1},{65,33},{97,65},{34,2},{66,34},{98,6... | collective-permute-start | bytes 196616 | tf_op jit(solution)/shard_map/ppermute | solution.py:20
  86.8 0.0 collective-permute-done.2
  86.8 0.1 constant_dynamic-update-slice_fusion.1
  86.9 3.4 %collective-permute-done.3 = bf16[16,2048]{1,0:T(8,128)(2,1)S(1)} collective-permute-done((bf16[16,2048]{1,0:T(8,128)(2,1)S(1)}, bf16[16,2048]{1,0:T(8,128)(2,1)S(1)}, u32[]{:S(2)}, u32[]{:S(2)}) %collective-permute-start.3) | collective-permute-done | bytes 65568 | tf_op jit(solution)/shard_map/ppermute | solution.py:20
  90.3 0.1 fusion.332
  90.4 7.7 %collective-permute-start.4 = (bf16[160,16]{1,0:T(8,128)(2,1)S(1)}, bf16[160,16]{1,0:T(8,128)(2,1)S(1)}, u32[]{:S(2)}, u32[]{:S(2)}) collective-permute-start(bf16[160,16]{1,0:T(8,128)(2,1)S(1)} %get-tuple-element.12), channel_id=1, source_target_pairs={{0,1},{1,2},{2,3},{3,4},{4,5},{5,6},{6,7},{7,8},{8,9},{9,10},{10,1... | collective-permute-start | bytes 15368 | tf_op jit(solution)/shard_map/ppermute | solution.py:19
  98.1 1.9 %collective-permute-start.5 = (bf16[160,16]{1,0:T(8,128)(2,1)S(1)}, bf16[160,16]{1,0:T(8,128)(2,1)S(1)}, u32[]{:S(2)}, u32[]{:S(2)}) collective-permute-start(bf16[160,16]{1,0:T(8,128)(2,1)S(1)} %get-tuple-element.11), channel_id=1, source_target_pairs={{1,0},{2,1},{3,2},{4,3},{5,4},{6,5},{7,6},{8,7},{9,8},{10,9},{11,1... | collective-permute-start | bytes 15368 | tf_op jit(solution)/shard_map/ppermute | solution.py:20
  100.1 0.7 fusion.337
  100.8 0.0 collective-permute-done.4
  100.8 4.8 %collective-permute-done.5 = bf16[160,16]{1,0:T(8,128)(2,1)S(1)} collective-permute-done((bf16[160,16]{1,0:T(8,128)(2,1)S(1)}, bf16[160,16]{1,0:T(8,128)(2,1)S(1)}, u32[]{:S(2)}, u32[]{:S(2)}) %collective-permute-start.5) | collective-permute-done | bytes 5152 | tf_op jit(solution)/shard_map/ppermute | solution.py:20
  105.6 0.7 concatenate.15
  106.3 21.3 %convolution_convert_fusion.2 = bf16[128,2080]{0,1:T(8,128)(2,1)S(1)} fusion(bf16[160,2080]{1,0:T(8,128)(2,1)S(1)} %concatenate.15, bf16[]{:T(256)} %bitcast.64, bf16[]{:T(256)} %bitcast.63, bf16[]{:T(256)} %bitcast.62, bf16[]{:T(256)} %bitcast.61, bf16[]{:T(256)} %bitcast.60, bf16[]{:T(256)} %bitcast.59, bf16[]{:T(256)} %bitcast.58, bf16[]{:T(256)} %bitcast.57, ...), kind=kOutput, calls=%fused_computation.5 | convolution fusion | flops 86835200 | bytes 1198146 | tf_op jit(solution)/shard_map/dot_general | solution.py:143
  127.6 0.0 copy-done
  127.7 0.3 fusion.213
  128.0 0.3 convolution_add_fusion.1
  128.4 0.3 convolution_add_fusion
  128.7 1.3 %copy.57 = f32[128,2048]{1,0:T(8,128)} copy(f32[128,2048]{0,1:T(8,128)S(1)} %bitcast.157) | data formatting | bytes 2097152
  (10 shorter events, 0.2 us)
Async XLA Ops:
  1.8 21.3 %collective-permute-start = (bf16[40,4096]{1,0:T(8,128)(2,1)S(1)}, bf16[40,4096]{1,0:T(8,128)(2,1)S(1)}, u32[]{:S(2)}, u32[]{:S(2)}) collective-permute-start(bf16[40,4096]{1,0:T(8,128)(2,1)S(1)} %get-tuple-element.15), channel_id=1, source_target_pairs={{0,1},{1,2},{2,3},{3,4},{4,5},{5,6},{6,7},{7,8},{8,9},{9,10},{10,1... | collective-permute-start | bytes 983048 | tf_op jit(solution)/shard_map/ppermute | solution.py:19
  4.1 19.0 %collective-permute-start.1 = (bf16[40,4096]{1,0:T(8,128)(2,1)S(1)}, bf16[40,4096]{1,0:T(8,128)(2,1)S(1)}, u32[]{:S(2)}, u32[]{:S(2)}) collective-permute-start(bf16[40,4096]{1,0:T(8,128)(2,1)S(1)} %get-tuple-element.16), channel_id=1, source_target_pairs={{1,0},{2,1},{3,2},{4,3},{5,4},{6,5},{7,6},{8,7},{9,8},{10,9},{11,1... | collective-permute-start | bytes 983048 | tf_op jit(solution)/shard_map/ppermute | solution.py:20
  38.1 11.2 %copy-start.1 = (f32[33]{0:T(128)S(1)}, f32[33]{0:T(128)}, u32[]{:S(2)}) copy-start(f32[33]{0:T(128)} %param.15) | copy-start | bytes 400
  38.1 11.3 %copy-start.2 = (f32[33]{0:T(128)S(1)}, f32[33]{0:T(128)}, u32[]{:S(2)}) copy-start(f32[33]{0:T(128)} %param.16) | copy-start | bytes 400
  38.1 38.5 %all-to-all-start = ((bf16[128,2,4160]{2,1,0:T(2,128)(2,1)}), bf16[128,2,4160]{2,1,0:T(2,128)(2,1)S(1)}, u32[]{:S(2)}, u32[]{:S(2)}) async-start(bf16[128,2,4160]{2,1,0:T(2,128)(2,1)} %pad_maximum_fusion), calls=%async_computation | async-start | bytes 4325376 | tf_op jit(solution)/shard_map/all_to_all | solution.py:33
  82.3 45.4 %copy-start = (bf16[16,8,16,128]{3,1,2,0:T(8,128)(2,1)}, bf16[16,8,16,128]{3,1,2,0:T(8,128)(2,1)S(1)}, u32[]{:S(2)}) copy-start(bf16[16,8,16,128]{3,1,2,0:T(8,128)(2,1)S(1)} %copy.83) | copy-start | bytes 1572868
  82.3 4.5 %collective-permute-start.2 = (bf16[16,2048]{1,0:T(8,128)(2,1)S(1)}, bf16[16,2048]{1,0:T(8,128)(2,1)S(1)}, u32[]{:S(2)}, u32[]{:S(2)}) collective-permute-start(bf16[16,2048]{1,0:T(8,128)(2,1)S(1)} %get-tuple-element.14), channel_id=1, source_target_pairs={{0,32},{32,64},{64,96},{1,33},{33,65},{65,97},{2,34},{34,66},{66,9... | collective-permute-start | bytes 196616 | tf_op jit(solution)/shard_map/ppermute | solution.py:19
  85.3 5.0 %collective-permute-start.3 = (bf16[16,2048]{1,0:T(8,128)(2,1)S(1)}, bf16[16,2048]{1,0:T(8,128)(2,1)S(1)}, u32[]{:S(2)}, u32[]{:S(2)}) collective-permute-start(bf16[16,2048]{1,0:T(8,128)(2,1)S(1)} %get-tuple-element.13), channel_id=1, source_target_pairs={{32,0},{64,32},{96,64},{33,1},{65,33},{97,65},{34,2},{66,34},{98,6... | collective-permute-start | bytes 196616 | tf_op jit(solution)/shard_map/ppermute | solution.py:20
  90.4 10.4 %collective-permute-start.4 = (bf16[160,16]{1,0:T(8,128)(2,1)S(1)}, bf16[160,16]{1,0:T(8,128)(2,1)S(1)}, u32[]{:S(2)}, u32[]{:S(2)}) collective-permute-start(bf16[160,16]{1,0:T(8,128)(2,1)S(1)} %get-tuple-element.12), channel_id=1, source_target_pairs={{0,1},{1,2},{2,3},{3,4},{4,5},{5,6},{6,7},{7,8},{8,9},{9,10},{10,1... | collective-permute-start | bytes 15368 | tf_op jit(solution)/shard_map/ppermute | solution.py:19
  98.1 7.4 %collective-permute-start.5 = (bf16[160,16]{1,0:T(8,128)(2,1)S(1)}, bf16[160,16]{1,0:T(8,128)(2,1)S(1)}, u32[]{:S(2)}, u32[]{:S(2)}) collective-permute-start(bf16[160,16]{1,0:T(8,128)(2,1)S(1)} %get-tuple-element.11), channel_id=1, source_target_pairs={{1,0},{2,1},{3,2},{4,3},{5,4},{6,5},{7,6},{8,7},{9,8},{10,9},{11,1... | collective-permute-start | bytes 15368 | tf_op jit(solution)/shard_map/ppermute | solution.py:20
where the time goes:
time: 131 us; the launch traced here: 130 us
  other arithmetic  36.6 us (28%)
  matrix products  32.3 us (25%)
  starting transfers between devices  29.1 us (22%)
  local copies, waits for them, and re-layouts  16.6 us (13%)
  waiting for transfers between devices  13.1 us (10%)
  between operations  2.3 us (2%)
    select_n x2, other arithmetic, band_matrix(): matrix = jnp.where(lag_index == position, weights[position], matrix)  24.8 us
    dot_general x1, matrix products, on_device(): jnp.dot(row_filter, framed, preferred_element_type=jnp.float32)  21.3 us
    ppermute x3, starting transfers between devices, extended_2(): before = lax.ppermute(last, axis, up)  12.3 us
    all_to_all x1, starting transfers between devices, sent_together(): lax.all_to_all(both, axis, split_axis=split_dim, concat_axis=concat_dim,...  11.2 us
    ppermute x3, waiting for transfers between devices, extended_2(): after = lax.ppermute(first, axis, down)  8.18 us
    ppermute x3, starting transfers between devices, extended_2(): after = lax.ppermute(first, axis, down)  5.57 us
    concatenate x1, other arithmetic, sent_together(): both = jnp.concatenate(arrays, axis=along)  5.16 us
    dot_general x1, matrix products, on_device(): jnp.dot(row_matrix, extended, preferred_element_type=jnp.float32)  5.06 us
  transfers between devices with their start and end apart: 7, of which 3 were waited for; matrix products, arithmetic and copies ran while one was open for 30% of the time, Pallas kernels for 0%

commit v1 on v0

v1 whole, which is shorter than its diff:
```python
import functools
import math

import jax
import jax.numpy as jnp
from jax import lax
from jax.experimental import pallas as pl
from jax.experimental.pallas import tpu as pltpu
from jax.sharding import PartitionSpec as P

MESH = pl.DeviceIdType.MESH
N = 128
ROWS = 64
COLS = 4096
EDGE = 48
EXT = ROWS + 2 * EDGE
TILES = COLS // 128
TAPS = 33
RIM = 16
PROWS, PCOLS = 128, 2048
F32, BF16, I32 = jnp.float32, jnp.bfloat16, jnp.int32


def iota(shape, dim):
    return lax.broadcasted_iota(I32, shape, dim)


def dot(a, b):
    return jnp.dot(a, b, preferred_element_type=F32)


def sinc(t):
    x = math.pi * t
    zero = t == 0.0
    x = jnp.where(zero, 1.0, x)
    return jnp.where(zero, 1.0, jnp.sin(x) / x)


def lanczos(f):
    k = iota((8, 128), 0)
    t = (3 - k).astype(F32) - f
    w = jnp.where(k < 6, sinc(t) * sinc(t / 3.0), 0.0)
    return w / jnp.sum(w, axis=0, keepdims=True)


def band(lag, weights):
    m = jnp.zeros(lag.shape, F32)
    for k, w in enumerate(weights):
        m = jnp.where(lag == k, w, m)
    return m


def kernel(
    exposure, offsets, fraction, idx_s, route_patch, route_slot, block_weight, kernel_rows, kernel_columns,
    coadded, matched,
    ext, rwb, wb, sbuf, rbuf, gf, nf, fr, sb, row_m, col_m, frow_m, fcol_m, a_m, meta,
    sem_in, sem_mg, sem_meta_s, sem_meta_r, sem_s, sem_r, sem_rim,
):
    v = lax.axis_index("visit")
    c = lax.axis_index("ccd")
    me = v * 32 + c
    core = lax.rem(c, 2)
    z = lax.rem(c // 2, 4)
    x = c // 8

    def peer(dv, dx, dz, dc):
        return (
            lax.rem(v + dv, 4),
            (lax.rem(x + dx, 4) * 4 + lax.rem(z + dz, 4)) * 2 + lax.rem(core + dc, 2),
        )

    def remote(src, dst, s, r, to):
        return pltpu.make_async_remote_copy(
            src_ref=src, dst_ref=dst, send_sem=s, recv_sem=r, device_id=to, device_id_type=MESH
        )

    c_next, c_prev = lax.rem(c + 1, 32), lax.rem(c + 31, 32)
    v_next, v_prev = lax.rem(v + 1, 4), lax.rem(v + 3, 4)

    bar = pltpu.get_barrier_semaphore()
    first = [peer(0, 0, 0, 1), (v, c_next), (v, c_prev)]
    for i in (1, 2, 3):
        first += [peer(i, 0, 0, 0), peer(0, i, 0, 0), peer(0, 0, i, 0)]
    for to in first:
        pl.semaphore_signal(bar, inc=1, device_id=to, device_id_type=MESH)

    own = pltpu.make_async_copy(exposure.at[0], ext.at[pl.ds(EDGE, ROWS)], sem_in)
    own.start()

    code = (route_patch[...] * 64 + route_slot[...]).astype(F32)
    meta[me] = jnp.concatenate([code, block_weight[...].astype(F32)], axis=1)

    pl.semaphore_wait(bar, len(first))

    margins = [
        remote(exposure.at[0, pl.ds(ROWS - EDGE, EDGE)], ext.at[pl.ds(0, EDGE)], sem_mg.at[0], sem_mg.at[1], (v, c_next)),
        remote(exposure.at[0, pl.ds(0, EDGE)], ext.at[pl.ds(EDGE + ROWS, EDGE)], sem_mg.at[2], sem_mg.at[3], (v, c_prev)),
    ]
    for copy in margins:
        copy.start()

    def stage(number, start, rows, peers):
        copies = []
        for i, to in enumerate(peers):
            piece = meta.at[pl.ds(start, rows)]
            copies.append(remote(piece, piece, sem_meta_s.at[number, i], sem_meta_r.at[number, i], to))
        for copy in copies:
            copy.start()
        return copies

    def finish(copies):
        for copy in copies:
            copy.wait()

    going = stage(0, me, 1, [peer(0, 0, 0, 1)])
    w_row = lanczos(fraction[0, 0, 0]).astype(BF16).astype(F32)
    lag = iota((ROWS, EXT), 1) - iota((ROWS, EXT), 0) - (EDGE - 3 - offsets[0, 0, 0])
    m = band(lag, [w_row[k : k + 1, 0:1] for k in range(6)])
    at = iota((ROWS, EXT), 1)
    outside = ((at < EDGE) & (c == 0)) | ((at >= EDGE + ROWS) & (c == 31))
    row_m[...] = jnp.where(outside, 0.0, m).astype(BF16)
    finish(going)

    going = stage(1, me - core, 2, [peer(0, 0, i, 0) for i in (1, 2, 3)])
    w_col = lanczos(fraction[0, 0, 1]).astype(BF16).astype(F32)
    lag = iota((384, 128), 0) - iota((384, 128), 1) - (125 - offsets[0, 0, 1])
    col_m[...] = band(lag, [w_col[k : k + 1, 0:1] for k in range(6)]).astype(BF16)
    finish(going)

    going = stage(2, v * 32 + x * 8, 8, [peer(0, i, 0, 0) for i in (1, 2, 3)])
    blank = jnp.zeros((64, 128), BF16)
    rwb[pl.ds(0, 64), :] = blank
    rwb[pl.ds(33 * 64, 64), :] = blank
    own.wait()
    finish(going)

    going = stage(3, v * 32, 32, [peer(i, 0, 0, 0) for i in (1, 2, 3)])
    for copy in margins:
        copy.wait()

    def row_pass(i, _):
        got = dot(row_m[...], ext[:, pl.ds(pl.multiple_of(i * 256, 256), 256)]).astype(BF16)
        at = pl.multiple_of(i * 128, 128)
        rwb[pl.ds(at + 64, 64), :] = got[:, :128]
        rwb[pl.ds(at + 128, 64), :] = got[:, 128:]
        return 0

    lax.fori_loop(0, TILES // 2, row_pass, 0, unroll=4)

    def column_pass(i, _):
        at = pl.multiple_of(i * 256, 256)
        three = jnp.concatenate([rwb[pl.ds(at + 64 * p, 256), :] for p in range(3)], axis=1)
        wb[pl.ds(i * 8, 8)] = dot(three, col_m[...]).astype(BF16).reshape(8, 32, 128)
        return 0

    lax.fori_loop(0, TILES // 4, column_pass, 0, unroll=2)
    finish(going)

    def pick(p, out, o):
        for k in range(2):
            out[o, pl.ds(32 * k, 32), :] = wb[idx_s[N * k + p]]

    def send(d, _):
        e = lax.rem(d * 37, N)
        pv, pc = peer(e // 32, lax.rem(e // 8, 4), lax.rem(e // 2, 4), lax.rem(e, 2))
        p = pv * 32 + pc
        pick(p, sbuf, d)
        remote(sbuf.at[d], rbuf.at[me], sem_s, sem_r, (pv, pc)).start()
        return 0

    lax.fori_loop(1, N, send, 0)
    pick(me, rbuf, me)

    lag = iota((PROWS, PROWS + 2 * RIM), 1) - iota((PROWS, PROWS + 2 * RIM), 0)
    m = band(lag, [kernel_rows[k] for k in range(TAPS)])
    at = iota((PROWS, PROWS + 2 * RIM), 1)
    outside = ((at < RIM) & (v == 0)) | ((at >= RIM + PROWS) & (v == 3))
    frow_m[...] = jnp.where(outside, 0.0, m).astype(BF16)
    lag = iota((384, 128), 0) - iota((384, 128), 1) - (128 - RIM)
    fcol_m[...] = band(lag, [kernel_columns[k] for k in range(TAPS)]).astype(BF16)

    every = meta[:, 0, :]
    weight = pltpu.roll(every, 64, 1)
    patch = jnp.floor(every * (1.0 / 64.0))
    slot = every - patch * 64.0
    lane = iota((N, N), 1)
    match = (patch == me.astype(F32)) & (lane < 64)
    earlier = jnp.where(iota((N, N), 0) < iota((N, N), 1), 1.0, 0.0).astype(BF16)
    rank = dot(jnp.where(match, 1.0, 0.0).astype(BF16), earlier)
    total = jnp.zeros((64, 1), F32)
    for k in range(2):
        chosen = match & (rank == float(k))
        s_k = jnp.sum(jnp.where(chosen, slot, 0.0), axis=1, keepdims=True)
        w_k = jnp.sum(jnp.where(chosen, weight, 0.0), axis=1, keepdims=True)
        table = jnp.where(lane.astype(F32) == s_k, w_k, 0.0).T[:64]
        total = total + jnp.sum(table, axis=1, keepdims=True)
        a_m[:, pl.ds(128 * k, 128)] = table.astype(BF16)
    scale = 1.0 / jnp.maximum(total, 1.0)

    pltpu.make_async_copy(sbuf.at[pl.ds(1, N - 1)], sbuf.at[pl.ds(1, N - 1)], sem_s).wait()
    pltpu.make_async_copy(rbuf.at[pl.ds(1, N - 1)], rbuf.at[pl.ds(1, N - 1)], sem_r).wait()

    def widen(s, _):
        gf[pl.ds(pl.multiple_of(s * 64, 64), 64), :] = rbuf[s].astype(F32)
        return 0

    lax.fori_loop(0, N, widen, 0, unroll=8)

    def coadd(i, _):
        pair = []
        for y in (2 * i, 2 * i + 1):
            halves = [gf[pl.ds(32 * k + y, N, stride=64), :] for k in range(2)]
            pair.append(jnp.concatenate(halves, axis=0).astype(BF16))
        got = dot(a_m[...], jnp.concatenate(pair, axis=1)) * scale
        nf[pl.ds(pl.multiple_of(i * 128, 128), 64), :] = got[:, :128]
        nf[pl.ds(pl.multiple_of(i * 128 + 64, 64), 64), :] = got[:, 128:]
        return 0

    lax.fori_loop(0, 16, coadd, 0, unroll=4)

    def lay(j, _):
        at = pl.multiple_of(j * 128, 128)
        for i in range(4):
            tile = nf[pl.ds(i * 16 + j, 32, stride=64), :].astype(BF16)
            fr[pl.ds(RIM + 32 * i, 32), pl.ds(at + 128, 128)] = tile
            coadded[pl.ds(32 * i, 32), pl.ds(at, 128)] = tile
        return 0

    lax.fori_loop(0, 16, lay, 0, unroll=4)

    top, bottom, centre = pl.ds(RIM, RIM), pl.ds(PROWS, RIM), pl.ds(RIM, PROWS)
    above, below = pl.ds(0, RIM), pl.ds(RIM + PROWS, RIM)
    west, east, across = pl.ds(128, 128), pl.ds(PCOLS, 128), pl.ds(128, PCOLS)
    left, right = pl.ds(0, 128), pl.ds(128 + PCOLS, 128)
    rims = []
    for n, (rows, cols, to_rows, to_cols, to) in enumerate(
        (
            (bottom, across, above, across, (v_next, c)),
            (top, across, below, across, (v_prev, c)),
            (centre, east, centre, left, (v, c_next)),
            (centre, west, centre, right, (v, c_prev)),
            (bottom, east, above, left, (v_next, c_next)),
            (bottom, west, above, right, (v_next, c_prev)),
            (top, east, below, left, (v_prev, c_next)),
            (top, west, below, right, (v_prev, c_prev)),
        )
    ):
        copy = remote(fr.at[rows, cols], fr.at[to_rows, to_cols], sem_rim.at[0, n], sem_rim.at[1, n], to)
        copy.start()
        rims.append(copy)
    for copy in rims:
        copy.wait()

    def smooth(i, _):
        got = dot(frow_m[...], fr[:, pl.ds(pl.multiple_of(i * 256, 256), 256)]).astype(BF16)
        at = pl.multiple_of(i * 256, 256)
        sb[pl.ds(at, 128), :] = got[:, :128]
        sb[pl.ds(at + 128, 128), :] = got[:, 128:]
        return 0

    lax.fori_loop(0, 9, smooth, 0, unroll=3)
    blank = jnp.zeros((128, 128), BF16)
    sb[pl.ds(0, 128), :] = jnp.where(c == 0, blank, sb[pl.ds(0, 128), :])
    sb[pl.ds(17 * 128, 128), :] = jnp.where(c == 31, blank, sb[pl.ds(17 * 128, 128), :])

    def match_columns(j, _):
        at = pl.multiple_of(j * 128, 128)
        three = jnp.concatenate([sb[pl.ds(at + 128 * p, 128), :] for p in range(3)], axis=1)
        matched[:, pl.ds(at, 128)] = dot(three, fcol_m[...])
        return 0

    lax.fori_loop(0, 16, match_columns, 0, unroll=4)


def on_device(exposure, offsets, fraction, route_patch, route_slot, block_weight, kernel_rows, kernel_columns):
    vmem = pl.BlockSpec(memory_space=pltpu.VMEM)
    smem = pl.BlockSpec(memory_space=pltpu.SMEM)
    dma = pltpu.SemaphoreType.DMA
    names = route_patch[0]
    block = jnp.arange(64)
    before = (names[None, :] == names[:, None]) & (block[None, :] < block[:, None])
    rank = jnp.sum(before.astype(I32), axis=1)
    target = names + N * rank
    at = (block % 32) * 2 + block // 32
    place = jnp.sum(jnp.where(jnp.arange(2 * N)[:, None] == target[None, :], at[None, :], 0), axis=1)
    return pl.pallas_call(
        kernel,
        out_shape=(
            jax.ShapeDtypeStruct((PROWS, PCOLS), BF16),
            jax.ShapeDtypeStruct((PROWS, PCOLS), F32),
        ),
        in_specs=[pl.BlockSpec(memory_space=pl.ANY), smem, smem, smem, vmem, vmem, vmem, smem, smem],
        out_specs=(vmem, vmem),
        scratch_shapes=[
            pltpu.VMEM((EXT, COLS), BF16),
            pltpu.VMEM(((TILES + 2) * 64, 128), BF16),
            pltpu.VMEM((TILES * 2, 32, 128), BF16),
            pltpu.VMEM((N, 64, 128), BF16),
            pltpu.VMEM((N, 64, 128), BF16),
            pltpu.VMEM((N * 64, 128), F32),
            pltpu.VMEM((32 * 64, 128), F32),
            pltpu.VMEM((PROWS + 2 * RIM, PCOLS + 256), BF16),
            pltpu.VMEM((18 * 128, 128), BF16),
            pltpu.VMEM((ROWS, EXT), BF16),
            pltpu.VMEM((384, 128), BF16),
            pltpu.VMEM((PROWS, PROWS + 2 * RIM), BF16),
            pltpu.VMEM((384, 128), BF16),
            pltpu.VMEM((64, 256), BF16),
            pltpu.VMEM((N, 1, 128), F32),
            dma,
            dma((4,)),
            dma((4, 3)),
            dma((4, 3)),
            dma,
            dma,
            dma((2, 8)),
        ],
        compiler_params=pltpu.CompilerParams(
            collective_id=0, has_side_effects=True, vmem_limit_bytes=40 * 2**20
        ),
    )(exposure, offsets, fraction, place, route_patch, route_slot, block_weight, kernel_rows, kernel_columns)


def solution(mesh):
    placed = (
        P("visit", "ccd", None),
        P("visit", "ccd", None),
        P("visit", "ccd", None),
        P("visit", "ccd"),
        P("visit", "ccd"),
        P("visit", "ccd"),
        P(),
        P(),
    )
    return jax.shard_map(
        on_device,
        mesh=mesh,
        in_specs=placed,
        out_specs=(P("visit", "ccd"), P("visit", "ccd")),
        check_vma=False,
    )
```

time: 131 us -> 61.6 us (0.47)
  the two profiles are of different devices: /device:TPU:97 before, /device:TPU:1 now
where the time goes in v1:
time: 61.6 us; the launch traced here: 61.3 us
  Pallas kernels  56.2 us (91%)
  local copies, waits for them, and re-layouts  4.04 us (7%)
  between operations  0.71 us (1%)
    pallas_call x1, Pallas kernels, on_device(): pl.pallas_call(kernel, out_shape=(jax.ShapeDtypeStruct((PROWS, PCOLS), BF...  56.2 us
    unnamed x18, local copies, waits for them, and re-layouts  4.04 us

profile of v1, /device:TPU:1, one launch (start us, length us, event | category | flops | bytes accessed | tf_op | source)
XLA Modules:
  0.0 61.3 jit_solution(17804349858713306875)
XLA Ops:
  0.6 0.0 copy-start.3
  0.6 0.6 %copy-done.3 = s32[1,64]{1,0:T(1,128)S(1)} copy-done((s32[1,64]{1,0:T(1,128)S(1)}, s32[1,64]{1,0:T(1,128)}, u32[]{:S(2)}) %copy-start.3) | copy-done | bytes 280
  1.3 0.2 convert_reduce_fusion
  1.5 0.0 copy-start.6
  1.5 0.0 copy-start.7
  1.5 0.0 copy-start.1
  1.5 0.0 copy-start.2
  1.5 0.0 copy-start.4
  1.5 0.0 copy-start.5
  1.6 0.1 select_reduce_fusion.idx_s
  1.7 0.5 copy-done.6
  2.1 0.0 copy-done.7
  2.1 0.0 copy-done.1
  2.2 0.0 copy-done.2
  2.2 0.0 copy-done.4
  2.2 0.0 copy-done.5
  2.2 0.0 copy-start
  2.2 1.0 %copy-done = bf16[1,64,4096]{2,1,0:T(8,128)(2,1)S(1)} copy-done((bf16[1,64,4096]{2,1,0:T(8,128)(2,1)S(1)}, bf16[1,64,4096]{2,1,0:T(8,128)(2,1)}, u32[]{:S(2)}) %copy-start) | copy-done | bytes 524312
  3.3 56.2 %shard_map.95 = (bf16[128,2048]{1,0:T(8,128)(2,1)S(1)}, f32[128,2048]{1,0:T(8,128)S(1)}) custom-call(bf16[1,64,4096]{2,1,0:T(8,128)(2,1)S(1)} %copy-done, s32[1,1,2]{2,1,0:T(1,128)S(1)} %copy-done.1, f32[1,1,2]{2,1,0:T(1,128)S(1)} %copy-done.2, s32[256]{0:T(256)S(1)} %select_reduce_fusion.idx_s, s32[1,64]{1,0:T(1,128)S(1)} %copy-done.3, ...), custom_call_target="tpu_custom_call" | custom-call | tf_op jit(solution)/shard_map/pallas_call | solution.py:286
  59.5 0.8 %copy.12 = bf16[128,2048]{1,0:T(8,128)(2,1)} copy(bf16[128,2048]{1,0:T(8,128)(2,1)S(1)} %get-tuple-element.4) | data formatting | bytes 1048576
  60.3 1.0 %copy.13 = f32[128,2048]{1,0:T(8,128)} copy(f32[128,2048]{1,0:T(8,128)S(1)} %get-tuple-element.5) | data formatting | bytes 2097152
  (2 shorter events, 0.0 us)
Async XLA Ops:
  0.6 0.7 %copy-start.3 = (s32[1,64]{1,0:T(1,128)S(1)}, s32[1,64]{1,0:T(1,128)}, u32[]{:S(2)}) copy-start(s32[1,64]{1,0:T(1,128)} %route_patch.1) | copy-start | bytes 772
  1.5 0.7 %copy-start.6 = (f32[33]{0:T(128)S(1)}, f32[33]{0:T(128)}, u32[]{:S(2)}) copy-start(f32[33]{0:T(128)} %kernel_rows.1) | copy-start | bytes 400
  1.5 0.7 %copy-start.7 = (f32[33]{0:T(128)S(1)}, f32[33]{0:T(128)}, u32[]{:S(2)}) copy-start(f32[33]{0:T(128)} %kernel_columns.1) | copy-start | bytes 400
  1.5 0.7 %copy-start.1 = (s32[1,1,2]{2,1,0:T(1,128)S(1)}, s32[1,1,2]{2,1,0:T(1,128)}, u32[]{:S(2)}) copy-start(s32[1,1,2]{2,1,0:T(1,128)} %offsets.1) | copy-start | bytes 28
  1.5 0.7 %copy-start.2 = (f32[1,1,2]{2,1,0:T(1,128)S(1)}, f32[1,1,2]{2,1,0:T(1,128)}, u32[]{:S(2)}) copy-start(f32[1,1,2]{2,1,0:T(1,128)} %fraction.1) | copy-start | bytes 28
  1.5 0.7 %copy-start.4 = (s32[1,64]{1,0:T(1,128)S(1)}, s32[1,64]{1,0:T(1,128)}, u32[]{:S(2)}) copy-start(s32[1,64]{1,0:T(1,128)} %route_slot.1) | copy-start | bytes 772
  1.5 0.7 %copy-start.5 = (bf16[1,64]{1,0:T(2,128)(2,1)S(1)}, bf16[1,64]{1,0:T(2,128)(2,1)}, u32[]{:S(2)}) copy-start(bf16[1,64]{1,0:T(2,128)(2,1)} %block_weight.1) | copy-start | bytes 388
  2.2 1.0 %copy-start = (bf16[1,64,4096]{2,1,0:T(8,128)(2,1)S(1)}, bf16[1,64,4096]{2,1,0:T(8,128)(2,1)}, u32[]{:S(2)}) copy-start(bf16[1,64,4096]{2,1,0:T(8,128)(2,1)} %exposure.1) | copy-start | bytes 1572868

commit v2 on v1

v2 whole, which is shorter than its diff:
```python
import functools
import math

import jax
import jax.numpy as jnp
from jax import lax
from jax.experimental import pallas as pl
from jax.experimental.pallas import tpu as pltpu
from jax.sharding import PartitionSpec as P

MESH = pl.DeviceIdType.MESH
N = 128
ROWS = 64
COLS = 4096
EDGE = 48
EXT = ROWS + 2 * EDGE
TILES = COLS // 128
TAPS = 33
RIM = 16
PROWS, PCOLS = 128, 2048
F32, BF16, I32 = jnp.float32, jnp.bfloat16, jnp.int32


def iota(shape, dim):
    return lax.broadcasted_iota(I32, shape, dim)


def dot(a, b):
    return jnp.dot(a, b, preferred_element_type=F32)


def sinc(t):
    x = math.pi * t
    zero = t == 0.0
    x = jnp.where(zero, 1.0, x)
    return jnp.where(zero, 1.0, jnp.sin(x) / x)


def lanczos(f):
    k = iota((8, 128), 0)
    t = (3 - k).astype(F32) - f
    w = jnp.where(k < 6, sinc(t) * sinc(t / 3.0), 0.0)
    return w / jnp.sum(w, axis=0, keepdims=True)


def band(lag, weights):
    m = jnp.zeros(lag.shape, F32)
    for k, w in enumerate(weights):
        m = jnp.where(lag == k, w, m)
    return m


def kernel(
    exposure, offsets_h, fraction_h, patch_h, slot_h, weight_h, krows_h, kcols_h,
    fr_h, frow_h, fcol_h,
    ext, rwb, wb, sbuf, rbuf, gf, nf, fr, row_m, col_m, frow_m, fcol_m, a_m, meta, offsets, fraction, route_patch, route_slot, block_weight, kernel_rows, kernel_columns, idx_v, idx_s,
    sem_in, sem_small, sem_mg, sem_meta, sem_s, sem_r, sem_rim, sem_out,
):
    v = lax.axis_index("visit")
    c = lax.axis_index("ccd")
    me = v * 32 + c
    core = lax.rem(c, 2)
    z = lax.rem(c // 2, 4)
    x = c // 8

    def peer(dv, dx, dz, dc):
        return (
            lax.rem(v + dv, 4),
            (lax.rem(x + dx, 4) * 4 + lax.rem(z + dz, 4)) * 2 + lax.rem(core + dc, 2),
        )

    def remote(src, dst, s, r, to):
        return pltpu.make_async_remote_copy(
            src_ref=src, dst_ref=dst, send_sem=s, recv_sem=r, device_id=to, device_id_type=MESH
        )

    c_next, c_prev = lax.rem(c + 1, 32), lax.rem(c + 31, 32)
    v_next, v_prev = lax.rem(v + 1, 4), lax.rem(v + 3, 4)

    bar = pltpu.get_barrier_semaphore()
    plane = [peer(0, i // 4, i % 4, 0) for i in range(1, 16)]
    line = [peer(i // 2, 0, 0, i % 2) for i in range(1, 8)]
    first = [(v, c_next), (v, c_prev)] + plane + line
    for to in first:
        pl.semaphore_signal(bar, inc=1, device_id=to, device_id_type=MESH)

    own = pltpu.make_async_copy(exposure.at[0], ext.at[pl.ds(EDGE, ROWS)], sem_in)
    own.start()
    small = [
        pltpu.make_async_copy(there, here, sem_small.at[n])
        for n, (there, here) in enumerate(
            (
                (patch_h, route_patch), (slot_h, route_slot), (weight_h, block_weight), (offsets_h, offsets),
                (fraction_h, fraction), (krows_h, kernel_rows), (kcols_h, kernel_columns),
            )
        )
    ]
    for copy in small:
        copy.start()
    for copy in small:
        copy.wait()

    dest_r = jnp.broadcast_to(route_patch[...], (64, 64))
    eye = iota((64, 64), 0) == iota((64, 64), 1)
    dest_c = jnp.sum(jnp.where(eye, dest_r, 0), axis=1, keepdims=True)
    before = (dest_r == dest_c) & (iota((64, 64), 1) < iota((64, 64), 0))
    rank_c = jnp.sum(jnp.where(before, 1, 0), axis=1, keepdims=True)
    b_c = iota((64, 128), 0)
    place = jnp.where(b_c < 32, 2 * b_c, 2 * b_c - 63)
    names = dest_c == iota((64, 128), 1)
    for k in range(2):
        chosen = jnp.where(names & (rank_c == k), place, 0)
        idx_v[pl.ds(k, 1), :] = jnp.sum(chosen, axis=0, keepdims=True)
    to_smem = pltpu.make_async_copy(idx_v, idx_s, sem_small.at[7])
    to_smem.start()

    code = (route_patch[...] * 64 + route_slot[...]).astype(F32)
    mine = v * 32 + core * 16 + x * 4 + z
    meta[mine] = jnp.concatenate([code, block_weight[...].astype(F32)], axis=1)

    pl.semaphore_wait(bar, len(first))

    margins = [
        remote(exposure.at[0, pl.ds(ROWS - EDGE, EDGE)], ext.at[pl.ds(0, EDGE)], sem_mg.at[0], sem_mg.at[1], (v, c_next)),
        remote(exposure.at[0, pl.ds(0, EDGE)], ext.at[pl.ds(EDGE + ROWS, EDGE)], sem_mg.at[2], sem_mg.at[3], (v, c_prev)),
    ]

    def stage(start, rows, peers, at):
        piece = meta.at[pl.ds(start, rows)]
        copies = [remote(piece, piece, sem_meta.at[0, at + i], sem_meta.at[1, at + i], to) for i, to in enumerate(peers)]
        for copy in copies:
            copy.start()
        return copies

    def finish(copies):
        for copy in copies:
            copy.wait()

    going = stage(mine, 1, plane, 0)
    for copy in margins:
        copy.start()
    w_row = lanczos(fraction[0, 0, 0]).astype(BF16).astype(F32)
    r = iota((ROWS, EXT), 0)
    row = jnp.where((r >= 16) & (r < 32), r + 16, jnp.where((r >= 32) & (r < 48), r - 16, r))
    lag = iota((ROWS, EXT), 1) - row - (EDGE - 3 - offsets[0, 0, 0])
    m = band(lag, [w_row[k : k + 1, 0:1] for k in range(6)])
    at = iota((ROWS, EXT), 1)
    outside = ((at < EDGE) & (c == 0)) | ((at >= EDGE + ROWS) & (c == 31))
    row_m[...] = jnp.where(outside, 0.0, m).astype(BF16)

    w_col = lanczos(fraction[0, 0, 1]).astype(BF16).astype(F32)
    lag = iota((384, 128), 0) - iota((384, 128), 1) - (125 - offsets[0, 0, 1])
    col_m[...] = band(lag, [w_col[k : k + 1, 0:1] for k in range(6)]).astype(BF16)
    finish(going)
    going = stage(v * 32 + core * 16, 16, line, 15)
    blank = jnp.zeros((64, 128), BF16)
    rwb[0] = blank
    rwb[TILES + 1] = blank
    own.wait()
    for copy in margins:
        copy.wait()

    def row_pass(i, _):
        got = dot(row_m[...], ext[:, pl.ds(pl.multiple_of(i * 256, 256), 256)]).astype(BF16)
        rwb[2 * i + 1] = got[:, :128]
        rwb[2 * i + 2] = got[:, 128:]
        return 0

    lax.fori_loop(0, TILES // 2, row_pass, 0, unroll=4)

    def column_pass(half, i, _):
        parts = [rwb[pl.ds(i * 8 + p, 8), pl.ds(32 * half, 32), :].reshape(256, 128) for p in range(3)]
        got = dot(jnp.concatenate(parts, axis=1), col_m[...]).astype(BF16)
        wb[half, pl.ds(i * 16, 16)] = got.reshape(16, 16, 128)
        return 0

    def pick(half, p, out, o):
        for k in range(2):
            out[half, o, pl.ds(16 * k, 16), :] = wb[half, idx_s[k, p]]

    def send(half, d, _):
        e = lax.rem(d * 37, N)
        pv, pc = peer(e // 32, lax.rem(e // 8, 4), lax.rem(e // 2, 4), lax.rem(e, 2))
        pick(half, pv * 32 + pc, sbuf, d)
        remote(sbuf.at[half, d], rbuf.at[half, me], sem_s.at[half], sem_r.at[half], (pv, pc)).start()
        return 0

    for half in range(2):
        lax.fori_loop(0, TILES // 8, functools.partial(column_pass, half), 0, unroll=2)
        if half == 0:
            to_smem.wait()
            finish(going)
        lax.fori_loop(1, N, functools.partial(send, half), 0)
        pick(half, me, rbuf, me)

    lag = iota((PROWS, PROWS + 2 * RIM), 1) - iota((PROWS, PROWS + 2 * RIM), 0)
    m = band(lag, [kernel_rows[k] for k in range(TAPS)])
    at = iota((PROWS, PROWS + 2 * RIM), 1)
    outside = ((at < RIM) & (v == 0)) | ((at >= RIM + PROWS) & (v == 3))
    frow_m[...] = jnp.where(outside, 0.0, m).astype(BF16)
    lag = iota((384, 128), 0) - iota((384, 128), 1) - (128 - RIM)
    fcol_m[...] = band(lag, [kernel_columns[k] for k in range(TAPS)]).astype(BF16)
    outs = [pltpu.make_async_copy(frow_m, frow_h, sem_out.at[0]), pltpu.make_async_copy(fcol_m, fcol_h, sem_out.at[1])]
    for copy in outs:
        copy.start()

    every = meta[:, 0, :]
    s_to = iota((N, N), 0)
    s_from = (s_to // 32) * 32 + (s_to % 2) * 16 + (s_to % 32) // 2
    swap = jnp.where(s_from == iota((N, N), 1), 1.0, 0.0).astype(BF16)
    weight = pltpu.roll(every, 64, 1)
    patch = jnp.floor(every * (1.0 / 64.0))
    slot = every - patch * 64.0
    lane = iota((N, N), 1)
    match = (patch == me.astype(F32)) & (lane < 64)
    earlier = jnp.where(iota((N, N), 0) < iota((N, N), 1), 1.0, 0.0).astype(BF16)
    rank = dot(jnp.where(match, 1.0, 0.0).astype(BF16), earlier)
    total = jnp.zeros((64, 1), F32)
    for k in range(2):
        chosen = match & (rank == float(k))
        s_k = jnp.sum(jnp.where(chosen, slot, 0.0), axis=1, keepdims=True)
        w_k = jnp.sum(jnp.where(chosen, weight, 0.0), axis=1, keepdims=True)
        table = dot(swap, jnp.where(lane.astype(F32) == s_k, w_k, 0.0).astype(BF16)).T[:64]
        total = total + jnp.sum(table, axis=1, keepdims=True)
        a_m[:, pl.ds(128 * k, 128)] = table.astype(BF16)
    scale = 1.0 / jnp.maximum(total, 1.0)

    top, bottom, centre = pl.ds(RIM, RIM), pl.ds(PROWS, RIM), pl.ds(RIM, PROWS)
    above, below = pl.ds(0, RIM), pl.ds(RIM + PROWS, RIM)
    west, east, across = pl.ds(128, 128), pl.ds(PCOLS, 128), pl.ds(128, PCOLS)
    left, right = pl.ds(0, 128), pl.ds(128 + PCOLS, 128)
    rims = [
        remote(fr.at[rows, cols], fr.at[to_rows, to_cols], sem_rim.at[0, n], sem_rim.at[1, n], to)
        for n, (rows, cols, to_rows, to_cols, to) in enumerate(
            (
                (top, across, below, across, (v_prev, c)),
                (top, east, below, left, (v_prev, c_next)),
                (top, west, below, right, (v_prev, c_prev)),
                (bottom, across, above, across, (v_next, c)),
                (centre, east, centre, left, (v, c_next)),
                (centre, west, centre, right, (v, c_prev)),
                (bottom, east, above, left, (v_next, c_next)),
                (bottom, west, above, right, (v_next, c_prev)),
            )
        )
    ]

    def widen(half, s, _):
        gf[pl.ds(pl.multiple_of(s * 32, 32), 32), :] = rbuf[half, s].astype(F32)
        return 0

    def coadd(i, _):
        pair = []
        for y in (2 * i, 2 * i + 1):
            halves = [gf[pl.ds(16 * k + y, N, stride=32), :] for k in range(2)]
            pair.append(jnp.concatenate(halves, axis=0).astype(BF16))
        got = dot(a_m[...], jnp.concatenate(pair, axis=1)) * scale
        nf[pl.ds(pl.multiple_of(i * 128, 128), 64), :] = got[:, :128]
        nf[pl.ds(pl.multiple_of(i * 128 + 64, 64), 64), :] = got[:, 128:]
        return 0

    def lay(half, j, _):
        at = pl.multiple_of(j * 128, 128)
        for i in range(4):
            tile = nf[pl.ds(i * 16 + j, 16, stride=64), :].astype(BF16)
            fr[pl.ds(RIM + 32 * i + 16 * half, 16), pl.ds(at + 128, 128)] = tile
        return 0

    for half in range(2):
        sent = sbuf.at[half, pl.ds(1, N - 1)]
        pltpu.make_async_copy(sent, sent, sem_r.at[half]).wait()
        lax.fori_loop(0, N, functools.partial(widen, half), 0, unroll=8)
        lax.fori_loop(0, 8, coadd, 0, unroll=4)
        lax.fori_loop(0, 16, functools.partial(lay, half), 0, unroll=4)
        for copy in rims[3 * half : 3 + 5 * half]:
            copy.start()

    for half in range(2):
        sent = sbuf.at[half, pl.ds(1, N - 1)]
        pltpu.make_async_copy(sent, sent, sem_s.at[half]).wait()
    for copy in rims:
        copy.wait()
    outs.append(pltpu.make_async_copy(fr, fr_h, sem_out.at[2]))
    outs[2].start()
    for copy in outs:
        copy.wait()


def filter_kernel(fr, frow_m, fcol_m, coadded, matched, sb, out, sem):
    c = lax.axis_index("ccd")
    lower = pltpu.make_async_copy(fr.at[pl.ds(RIM, PROWS), pl.ds(128, PCOLS)], coadded, sem.at[0])
    lower.start()

    def smooth(i, _):
        got = dot(frow_m[...], fr[:, pl.ds(pl.multiple_of(i * 256, 256), 256)]).astype(BF16)
        at = pl.multiple_of(i * 256, 256)
        sb[pl.ds(at, 128), :] = got[:, :128]
        sb[pl.ds(at + 128, 128), :] = got[:, 128:]
        return 0

    lax.fori_loop(0, 9, smooth, 0, unroll=3)
    blank = jnp.zeros((128, 128), BF16)
    sb[pl.ds(0, 128), :] = jnp.where(c == 0, blank, sb[pl.ds(0, 128), :])
    sb[pl.ds(17 * 128, 128), :] = jnp.where(c == 31, blank, sb[pl.ds(17 * 128, 128), :])

    copies = []
    for half in range(2):
        for j in range(8 * half, 8 * half + 8):
            three = jnp.concatenate([sb[pl.ds((j + p) * 128, 128), :] for p in range(3)], axis=1)
            out[:, pl.ds(j * 128, 128)] = dot(three, fcol_m[...])
        cols = pl.ds(half * 1024, 1024)
        copies.append(pltpu.make_async_copy(out.at[:, cols], matched.at[:, cols], sem.at[1 + half]))
        copies[-1].start()
    for copy in [lower] + copies:
        copy.wait()


def on_device(exposure, offsets, fraction, route_patch, route_slot, block_weight, kernel_rows, kernel_columns):
    hbm = pl.BlockSpec(memory_space=pltpu.HBM)
    vmem = pl.BlockSpec(memory_space=pltpu.VMEM)
    dma = pltpu.SemaphoreType.DMA
    framed = pl.pallas_call(
        kernel,
        out_shape=(
            jax.ShapeDtypeStruct((PROWS + 2 * RIM, PCOLS + 256), BF16),
            jax.ShapeDtypeStruct((PROWS, PROWS + 2 * RIM), BF16),
            jax.ShapeDtypeStruct((384, 128), BF16),
        ),
        in_specs=[hbm] * 8,
        out_specs=(hbm,) * 3,
        scratch_shapes=[
            pltpu.VMEM((EXT, COLS), BF16),
            pltpu.VMEM((TILES + 2, 64, 128), BF16),
            pltpu.VMEM((2, TILES * 2, 16, 128), BF16),
            pltpu.VMEM((2, N, 32, 128), BF16),
            pltpu.VMEM((2, N, 32, 128), BF16),
            pltpu.VMEM((N * 32, 128), F32),
            pltpu.VMEM((16 * 64, 128), F32),
            pltpu.VMEM((PROWS + 2 * RIM, PCOLS + 256), BF16),
            pltpu.VMEM((ROWS, EXT), BF16),
            pltpu.VMEM((384, 128), BF16),
            pltpu.VMEM((PROWS, PROWS + 2 * RIM), BF16),
            pltpu.VMEM((384, 128), BF16),
            pltpu.VMEM((64, 256), BF16),
            pltpu.VMEM((N, 1, 128), F32),
            pltpu.SMEM((1, 1, 2), I32),
            pltpu.SMEM((1, 1, 2), F32),
            pltpu.VMEM((1, 64), I32),
            pltpu.VMEM((1, 64), I32),
            pltpu.VMEM((1, 64), BF16),
            pltpu.SMEM((TAPS,), F32),
            pltpu.SMEM((TAPS,), F32),
            pltpu.VMEM((2, 128), I32),
            pltpu.SMEM((2, 128), I32),
            dma,
            dma((8,)),
            dma((4,)),
            dma((2, 22)),
            dma((2,)),
            dma((2,)),
            dma((2, 8)),
            dma((3,)),
        ],
        compiler_params=pltpu.CompilerParams(
            collective_id=0, has_side_effects=True, vmem_limit_bytes=60 * 2**20
        ),
    )(exposure, offsets, fraction, route_patch, route_slot, block_weight, kernel_rows, kernel_columns)
    return pl.pallas_call(
        filter_kernel,
        out_shape=(
            jax.ShapeDtypeStruct((PROWS, PCOLS), BF16),
            jax.ShapeDtypeStruct((PROWS, PCOLS), F32),
        ),
        in_specs=[vmem] * 3,
        out_specs=(hbm, hbm),
        scratch_shapes=[
            pltpu.VMEM((18 * 128, 128), BF16),
            pltpu.VMEM((PROWS, PCOLS), F32),
            dma((3,)),
        ],
        compiler_params=pltpu.CompilerParams(vmem_limit_bytes=60 * 2**20),
    )(*framed)


def solution(mesh):
    placed = (
        P("visit", "ccd", None),
        P("visit", "ccd", None),
        P("visit", "ccd", None),
        P("visit", "ccd"),
        P("visit", "ccd"),
        P("visit", "ccd"),
        P(),
        P(),
    )
    return jax.shard_map(
        on_device,
        mesh=mesh,
        in_specs=placed,
        out_specs=(P("visit", "ccd"), P("visit", "ccd")),
        check_vma=False,
    )
```

time: 61.6 us -> 56.1 us (0.911)
  local copies, waits for them, and re-layouts: 4.04 us -> 0 us
  Pallas kernels: 56.2 us -> 55.4 us
    unnamed x18 -> x0, local copies, waits for them, and re-layouts: 4.04 us -> none
    pallas_call x1 -> x2, Pallas kernels: 56.2 us -> 55.4 us  [the longest x1 52.2 us: on_device(): pl.pallas_call(kernel, out_shape=(jax.ShapeDtypeStruct((PROWS + 2 * RIM,...]
where the time goes in v2:
time: 56.1 us; the launch traced here: 56 us
  Pallas kernels  55.4 us (99%)
  between operations  0.64 us (1%)
    pallas_call x1, Pallas kernels, on_device(): pl.pallas_call(kernel, out_shape=(jax.ShapeDtypeStruct((PROWS + 2 * RIM,...  52.2 us
    pallas_call x1, Pallas kernels, on_device(): pl.pallas_call(filter_kernel, out_shape=(jax.ShapeDtypeStruct((PROWS, PCO...  3.17 us

profile of v2, /device:TPU:1, one launch (start us, length us, event | category | flops | bytes accessed | tf_op | source)
XLA Modules:
  0.0 56.0 jit_solution(12935811022675943731)
XLA Ops:
  0.6 52.2 %shard_map.95 = (bf16[160,2304]{1,0:T(8,128)(2,1)}, bf16[128,160]{1,0:T(8,128)(2,1)}, bf16[384,128]{1,0:T(8,128)(2,1)}) custom-call(bf16[1,64,4096]{2,1,0:T(8,128)(2,1)} %exposure.1, s32[1,1,2]{2,1,0:T(1,128)} %offsets_h.1, f32[1,1,2]{2,1,0:T(1,128)} %fraction_h.1, s32[1,64]{1,0:T(1,128)} %patch_h.1, s32[1,64]{1,0:T(1,128)} %slot_h.1, ...), custom_call_target="tpu_custom_call" | custom-call | tf_op jit(solution)/shard_map/pallas_call | solution.py:322
  52.8 3.2 %shard_map.96 = (bf16[128,2048]{1,0:T(8,128)(2,1)}, f32[128,2048]{1,0:T(8,128)}) custom-call(bf16[160,2304]{1,0:T(8,128)(2,1)} %get-tuple-element.5.fr, bf16[128,160]{1,0:T(8,128)(2,1)} %get-tuple-element.6.frow_m, bf16[384,128]{1,0:T(8,128)(2,1)} %get-tuple-element.7.fcol_m), custom_call_target="tpu_custom_call" | custom-call | tf_op jit(solution)/shard_map/pallas_call | solution.py:368

commit v3 on v2

--- a/solution.py
+++ b/solution.py
@@ -16,6 +16,7 @@
 EXT = ROWS + 2 * EDGE
 TILES = COLS // 128
 TAPS = 33
+PARTS = 4
 RIM = 16
 PROWS, PCOLS = 128, 2048
 F32, BF16, I32 = jnp.float32, jnp.bfloat16, jnp.int32
@@ -54,7 +55,7 @@
     exposure, offsets_h, fraction_h, patch_h, slot_h, weight_h, krows_h, kcols_h,
     fr_h, frow_h, fcol_h,
     ext, rwb, wb, sbuf, rbuf, gf, nf, fr, row_m, col_m, frow_m, fcol_m, a_m, meta, offsets, fraction, route_patch, route_slot, block_weight, kernel_rows, kernel_columns, idx_v, idx_s,
-    sem_in, sem_small, sem_mg, sem_meta, sem_s, sem_r, sem_rim, sem_out,
+    sem_in, sem_small, sem_mg, sem_round, sem_meta, sem_s, sem_r, sem_rim, sem_out,
 ):
     v = lax.axis_index("visit")
     c = lax.axis_index("ccd")
@@ -97,9 +98,43 @@
     ]
     for copy in small:
         copy.start()
+    pl.semaphore_wait(bar, len(first))
+    for to in line:
+        pl.semaphore_signal(sem_round, inc=1, device_id=to, device_id_type=MESH)
+
+    margins = []
+    for n in range(PARTS):
+        cols = pl.ds(n * (COLS // PARTS), COLS // PARTS)
+        low, high = exposure.at[0, pl.ds(ROWS - EDGE, EDGE), cols], exposure.at[0, pl.ds(0, EDGE), cols]
+        margins.append(
+            [
+                remote(low, ext.at[pl.ds(0, EDGE), cols], sem_mg.at[0, n], sem_mg.at[1, n], (v, c_next)),
+                remote(high, ext.at[pl.ds(EDGE + ROWS, EDGE), cols], sem_mg.at[2, n], sem_mg.at[3, n], (v, c_prev)),
+            ]
+        )
+
+    for pair in margins:
+        for copy in pair:
+            copy.start()
+
     for copy in small:
         copy.wait()
 
+    code = (route_patch[...] * 64 + route_slot[...]).astype(F32)
+    meta[me] = jnp.concatenate([code, block_weight[...].astype(F32)], axis=1)
+
+    w_row = lanczos(fraction[0, 0, 0]).astype(BF16).astype(F32)
+    r = iota((ROWS, EXT), 0)
+    row = jnp.where((r >= 16) & (r < 32), r + 16, jnp.where((r >= 32) & (r < 48), r - 16, r))
+    lag = iota((ROWS, EXT), 1) - row - (EDGE - 3 - offsets[0, 0, 0])
+    m = band(lag, [w_row[k : k + 1, 0:1] for k in range(6)])
+    at = iota((ROWS, EXT), 1)
+    outside = ((at < EDGE) & (c == 0)) | ((at >= EDGE + ROWS) & (c == 31))
+    row_m[...] = jnp.where(outside, 0.0, m).astype(BF16)
+
+    w_col = lanczos(fraction[0, 0, 1]).astype(BF16).astype(F32)
+    lag = iota((384, 128), 0) - iota((384, 128), 1) - (125 - offsets[0, 0, 1])
+    col_m[...] = band(lag, [w_col[k : k + 1, 0:1] for k in range(6)]).astype(BF16)
     dest_r = jnp.broadcast_to(route_patch[...], (64, 64))
     eye = iota((64, 64), 0) == iota((64, 64), 1)
     dest_c = jnp.sum(jnp.where(eye, dest_r, 0), axis=1, keepdims=True)
@@ -114,51 +149,10 @@
     to_smem = pltpu.make_async_copy(idx_v, idx_s, sem_small.at[7])
     to_smem.start()
 
-    code = (route_patch[...] * 64 + route_slot[...]).astype(F32)
-    mine = v * 32 + core * 16 + x * 4 + z
-    meta[mine] = jnp.concatenate([code, block_weight[...].astype(F32)], axis=1)
-
-    pl.semaphore_wait(bar, len(first))
-
-    margins = [
-        remote(exposure.at[0, pl.ds(ROWS - EDGE, EDGE)], ext.at[pl.ds(0, EDGE)], sem_mg.at[0], sem_mg.at[1], (v, c_next)),
-        remote(exposure.at[0, pl.ds(0, EDGE)], ext.at[pl.ds(EDGE + ROWS, EDGE)], sem_mg.at[2], sem_mg.at[3], (v, c_prev)),
-    ]
-
-    def stage(start, rows, peers, at):
-        piece = meta.at[pl.ds(start, rows)]
-        copies = [remote(piece, piece, sem_meta.at[0, at + i], sem_meta.at[1, at + i], to) for i, to in enumerate(peers)]
-        for copy in copies:
-            copy.start()
-        return copies
-
-    def finish(copies):
-        for copy in copies:
-            copy.wait()
-
-    going = stage(mine, 1, plane, 0)
-    for copy in margins:
-        copy.start()
-    w_row = lanczos(fraction[0, 0, 0]).astype(BF16).astype(F32)
-    r = iota((ROWS, EXT), 0)
-    row = jnp.where((r >= 16) & (r < 32), r + 16, jnp.where((r >= 32) & (r < 48), r - 16, r))
-    lag = iota((ROWS, EXT), 1) - row - (EDGE - 3 - offsets[0, 0, 0])
-    m = band(lag, [w_row[k : k + 1, 0:1] for k in range(6)])
-    at = iota((ROWS, EXT), 1)
-    outside = ((at < EDGE) & (c == 0)) | ((at >= EDGE + ROWS) & (c == 31))
-    row_m[...] = jnp.where(outside, 0.0, m).astype(BF16)
-
-    w_col = lanczos(fraction[0, 0, 1]).astype(BF16).astype(F32)
-    lag = iota((384, 128), 0) - iota((384, 128), 1) - (125 - offsets[0, 0, 1])
-    col_m[...] = band(lag, [w_col[k : k + 1, 0:1] for k in range(6)]).astype(BF16)
-    finish(going)
-    going = stage(v * 32 + core * 16, 16, line, 15)
     blank = jnp.zeros((64, 128), BF16)
     rwb[0] = blank
     rwb[TILES + 1] = blank
     own.wait()
-    for copy in margins:
-        copy.wait()
 
     def row_pass(i, _):
         got = dot(row_m[...], ext[:, pl.ds(pl.multiple_of(i * 256, 256), 256)]).astype(BF16)
@@ -166,7 +160,11 @@
         rwb[2 * i + 2] = got[:, 128:]
         return 0
 
-    lax.fori_loop(0, TILES // 2, row_pass, 0, unroll=4)
+    for n, pair in enumerate(margins):
+        for copy in pair:
+            copy.wait()
+        per = TILES // 2 // PARTS
+        lax.fori_loop(n * per, (n + 1) * per, row_pass, 0, unroll=4)
 
     def column_pass(half, i, _):
         parts = [rwb[pl.ds(i * 8 + p, 8), pl.ds(32 * half, 32), :].reshape(256, 128) for p in range(3)]
@@ -179,17 +177,19 @@
             out[half, o, pl.ds(16 * k, 16), :] = wb[half, idx_s[k, p]]
 
     def send(half, d, _):
-        e = lax.rem(d * 37, N)
+        e = lax.rem(d * 53, N)
         pv, pc = peer(e // 32, lax.rem(e // 8, 4), lax.rem(e // 2, 4), lax.rem(e, 2))
         pick(half, pv * 32 + pc, sbuf, d)
         remote(sbuf.at[half, d], rbuf.at[half, me], sem_s.at[half], sem_r.at[half], (pv, pc)).start()
+        if half == 0:
+            remote(meta.at[me], meta.at[me], sem_meta.at[0], sem_meta.at[1], (pv, pc)).start()
         return 0
 
     for half in range(2):
         lax.fori_loop(0, TILES // 8, functools.partial(column_pass, half), 0, unroll=2)
         if half == 0:
             to_smem.wait()
-            finish(going)
+            pl.semaphore_wait(sem_round, len(line))
         lax.fori_loop(1, N, functools.partial(send, half), 0)
         pick(half, me, rbuf, me)
 
@@ -204,10 +204,9 @@
     for copy in outs:
         copy.start()
 
+    for i in range(2):
+        pltpu.make_async_copy(meta.at[pl.ds(0, N - 1)], meta.at[pl.ds(0, N - 1)], sem_meta.at[i]).wait()
     every = meta[:, 0, :]
-    s_to = iota((N, N), 0)
-    s_from = (s_to // 32) * 32 + (s_to % 2) * 16 + (s_to % 32) // 2
-    swap = jnp.where(s_from == iota((N, N), 1), 1.0, 0.0).astype(BF16)
     weight = pltpu.roll(every, 64, 1)
     patch = jnp.floor(every * (1.0 / 64.0))
     slot = every - patch * 64.0
@@ -220,7 +219,7 @@
         chosen = match & (rank == float(k))
         s_k = jnp.sum(jnp.where(chosen, slot, 0.0), axis=1, keepdims=True)
         w_k = jnp.sum(jnp.where(chosen, weight, 0.0), axis=1, keepdims=True)
-        table = dot(swap, jnp.where(lane.astype(F32) == s_k, w_k, 0.0).astype(BF16)).T[:64]
+        table = jnp.where(lane.astype(F32) == s_k, w_k, 0.0).T[:64]
         total = total + jnp.sum(table, axis=1, keepdims=True)
         a_m[:, pl.ds(128 * k, 128)] = table.astype(BF16)
     scale = 1.0 / jnp.maximum(total, 1.0)
@@ -246,23 +245,23 @@
     ]
 
     def widen(half, s, _):
-        gf[pl.ds(pl.multiple_of(s * 32, 32), 32), :] = rbuf[half, s].astype(F32)
+        gf[pl.ds(pl.multiple_of(s * 40, 8), 32), :] = rbuf[half, s].astype(F32)
         return 0
 
     def coadd(i, _):
         pair = []
         for y in (2 * i, 2 * i + 1):
-            halves = [gf[pl.ds(16 * k + y, N, stride=32), :] for k in range(2)]
+            halves = [gf[pl.ds(16 * k + y, N, stride=40), :] for k in range(2)]
             pair.append(jnp.concatenate(halves, axis=0).astype(BF16))
         got = dot(a_m[...], jnp.concatenate(pair, axis=1)) * scale
-        nf[pl.ds(pl.multiple_of(i * 128, 128), 64), :] = got[:, :128]
-        nf[pl.ds(pl.multiple_of(i * 128 + 64, 64), 64), :] = got[:, 128:]
+        nf[pl.ds(pl.multiple_of(i * 144, 8), 64), :] = got[:, :128]
+        nf[pl.ds(pl.multiple_of(i * 144 + 72, 8), 64), :] = got[:, 128:]
         return 0
 
     def lay(half, j, _):
         at = pl.multiple_of(j * 128, 128)
         for i in range(4):
-            tile = nf[pl.ds(i * 16 + j, 16, stride=64), :].astype(BF16)
+            tile = nf[pl.ds(i * 16 + j, 16, stride=72), :].astype(BF16)
             fr[pl.ds(RIM + 32 * i + 16 * half, 16), pl.ds(at + 128, 128)] = tile
         return 0
 
@@ -278,46 +277,61 @@
     for half in range(2):
         sent = sbuf.at[half, pl.ds(1, N - 1)]
         pltpu.make_async_copy(sent, sent, sem_s.at[half]).wait()
+    everywhere = pl.ds(0, PCOLS + 256)
+    parts = ((centre, across), (above, everywhere), (below, everywhere), (centre, left), (centre, right))
+    for n, where in enumerate(parts):
+        outs.append(pltpu.make_async_copy(fr.at[where], fr_h.at[where], sem_out.at[2 + n]))
+    outs[2].start()
     for copy in rims:
         copy.wait()
-    outs.append(pltpu.make_async_copy(fr, fr_h, sem_out.at[2]))
-    outs[2].start()
+    for copy in outs[3:]:
+        copy.start()
     for copy in outs:
         copy.wait()
 
 
-def filter_kernel(fr, frow_m, fcol_m, coadded, matched, sb, out, sem):
+def filter_kernel(fr_h, frow_h, fcol_h, coadded, matched, fr, frow_m, fcol_m, sb, out, sem):
     c = lax.axis_index("ccd")
-    lower = pltpu.make_async_copy(fr.at[pl.ds(RIM, PROWS), pl.ds(128, PCOLS)], coadded, sem.at[0])
-    lower.start()
-
-    def smooth(i, _):
-        got = dot(frow_m[...], fr[:, pl.ds(pl.multiple_of(i * 256, 256), 256)]).astype(BF16)
-        at = pl.multiple_of(i * 256, 256)
-        sb[pl.ds(at, 128), :] = got[:, :128]
-        sb[pl.ds(at + 128, 128), :] = got[:, 128:]
-        return 0
-
-    lax.fori_loop(0, 9, smooth, 0, unroll=3)
-    blank = jnp.zeros((128, 128), BF16)
-    sb[pl.ds(0, 128), :] = jnp.where(c == 0, blank, sb[pl.ds(0, 128), :])
-    sb[pl.ds(17 * 128, 128), :] = jnp.where(c == 31, blank, sb[pl.ds(17 * 128, 128), :])
-
-    copies = []
-    for half in range(2):
-        for j in range(8 * half, 8 * half + 8):
+    ins = [pltpu.make_async_copy(frow_h, frow_m, sem.at[0]), pltpu.make_async_copy(fcol_h, fcol_m, sem.at[1])]
+    for n in range(3):
+        cols = pl.ds(n * 768, 768)
+        ins.append(pltpu.make_async_copy(fr_h.at[:, cols], fr.at[:, cols], sem.at[2 + n]))
+    for copy in ins:
+        copy.start()
+    outs = []
+    ins[0].wait()
+    ins[1].wait()
+
+    done = 0
+    for n in range(3):
+        ins[2 + n].wait()
+        left, right = max(768 * n, 128), min(768 * n + 768, 128 + PCOLS)
+        centre = fr.at[pl.ds(RIM, PROWS), pl.ds(left, right - left)]
+        outs.append(pltpu.make_async_copy(centre, coadded.at[:, pl.ds(left - 128, right - left)], sem.at[5 + n]))
+        outs[-1].start()
+        for i in range(3 * n, 3 * n + 3):
+            got = dot(frow_m[...], fr[:, pl.ds(i * 256, 256)]).astype(BF16)
+            for half in range(2):
+                tile = got[:, 128 * half : 128 * half + 128]
+                if i == 0 and half == 0:
+                    tile = jnp.where(c == 0, jnp.zeros_like(tile), tile)
+                if i == 8 and half == 1:
+                    tile = jnp.where(c == 31, jnp.zeros_like(tile), tile)
+                sb[pl.ds(i * 256 + half * 128, 128), :] = tile
+        ready = 6 * n + 4
+        for j in range(done, ready):
             three = jnp.concatenate([sb[pl.ds((j + p) * 128, 128), :] for p in range(3)], axis=1)
             out[:, pl.ds(j * 128, 128)] = dot(three, fcol_m[...])
-        cols = pl.ds(half * 1024, 1024)
-        copies.append(pltpu.make_async_copy(out.at[:, cols], matched.at[:, cols], sem.at[1 + half]))
-        copies[-1].start()
-    for copy in [lower] + copies:
+        cols = pl.ds(done * 128, (ready - done) * 128)
+        outs.append(pltpu.make_async_copy(out.at[:, cols], matched.at[:, cols], sem.at[8 + n]))
+        outs[-1].start()
+        done = ready
+    for copy in outs:
         copy.wait()
 
 
 def on_device(exposure, offsets, fraction, route_patch, route_slot, block_weight, kernel_rows, kernel_columns):
     hbm = pl.BlockSpec(memory_space=pltpu.HBM)
-    vmem = pl.BlockSpec(memory_space=pltpu.VMEM)
     dma = pltpu.SemaphoreType.DMA
     framed = pl.pallas_call(
         kernel,
@@ -334,8 +348,8 @@
             pltpu.VMEM((2, TILES * 2, 16, 128), BF16),
             pltpu.VMEM((2, N, 32, 128), BF16),
             pltpu.VMEM((2, N, 32, 128), BF16),
-            pltpu.VMEM((N * 32, 128), F32),
-            pltpu.VMEM((16 * 64, 128), F32),
+            pltpu.VMEM((N * 40, 128), F32),
+            pltpu.VMEM((16 * 72, 128), F32),
             pltpu.VMEM((PROWS + 2 * RIM, PCOLS + 256), BF16),
             pltpu.VMEM((ROWS, EXT), BF16),
             pltpu.VMEM((384, 128), BF16),
@@ -354,12 +368,13 @@
             pltpu.SMEM((2, 128), I32),
             dma,
             dma((8,)),
-            dma((4,)),
-            dma((2, 22)),
+            dma((4, PARTS)),
+            pltpu.SemaphoreType.REGULAR,
+            dma((2,)),
             dma((2,)),
             dma((2,)),
             dma((2, 8)),
-            dma((3,)),
+            dma((7,)),
         ],
         compiler_params=pltpu.CompilerParams(
             collective_id=0, has_side_effects=True, vmem_limit_bytes=60 * 2**20
@@ -371,12 +386,15 @@
             jax.ShapeDtypeStruct((PROWS, PCOLS), BF16),
             jax.ShapeDtypeStruct((PROWS, PCOLS), F32),
         ),
-        in_specs=[vmem] * 3,
+        in_specs=[hbm] * 3,
         out_specs=(hbm, hbm),
         scratch_shapes=[
+            pltpu.VMEM((PROWS + 2 * RIM, PCOLS + 256), BF16),
+            pltpu.VMEM((PROWS, PROWS + 2 * RIM), BF16),
+            pltpu.VMEM((384, 128), BF16),
             pltpu.VMEM((18 * 128, 128), BF16),
             pltpu.VMEM((PROWS, PCOLS), F32),
-            dma((3,)),
+            dma((11,)),
         ],
         compiler_params=pltpu.CompilerParams(vmem_limit_bytes=60 * 2**20),
     )(*framed)

time: 56.1 us -> 53.7 us (0.957)
  Pallas kernels: 55.4 us -> 53 us
    pallas_call x1, Pallas kernels: 52.2 us -> 49.8 us  [on_device(): pl.pallas_call(kernel, out_shape=(jax.ShapeDtypeStruct((PROWS + 2 * RIM,...]
where the time goes in v3:
time: 53.7 us; the launch traced here: 53.6 us
  Pallas kernels  53 us (99%)
  between operations  0.64 us (1%)
    pallas_call x1, Pallas kernels, on_device(): pl.pallas_call(kernel, out_shape=(jax.ShapeDtypeStruct((PROWS + 2 * RIM,...  49.8 us
    pallas_call x1, Pallas kernels, on_device(): pl.pallas_call(filter_kernel, out_shape=(jax.ShapeDtypeStruct((PROWS, PCO...  3.13 us

profile of v3, /device:TPU:1, one launch (start us, length us, event | category | flops | bytes accessed | tf_op | source)
XLA Modules:
  0.0 53.6 jit_solution(16624837982763852004)
XLA Ops:
  0.6 49.8 %shard_map.95 = (bf16[160,2304]{1,0:T(8,128)(2,1)}, bf16[128,160]{1,0:T(8,128)(2,1)}, bf16[384,128]{1,0:T(8,128)(2,1)}) custom-call(bf16[1,64,4096]{2,1,0:T(8,128)(2,1)} %exposure.1, s32[1,1,2]{2,1,0:T(1,128)} %offsets_h.1, f32[1,1,2]{2,1,0:T(1,128)} %fraction_h.1, s32[1,64]{1,0:T(1,128)} %patch_h.1, s32[1,64]{1,0:T(1,128)} %slot_h.1, ...), custom_call_target="tpu_custom_call" | custom-call | tf_op jit(solution)/shard_map/pallas_call | solution.py:336
  50.5 3.1 %shard_map.96 = (bf16[128,2048]{1,0:T(8,128)(2,1)}, f32[128,2048]{1,0:T(8,128)}) custom-call(bf16[160,2304]{1,0:T(8,128)(2,1)} %get-tuple-element.5.fr_h, bf16[128,160]{1,0:T(8,128)(2,1)} %get-tuple-element.6.frow_h, bf16[384,128]{1,0:T(8,128)(2,1)} %get-tuple-element.7.fcol_h), custom_call_target="tpu_custom_call" | custom-call | tf_op jit(solution)/shard_map/pallas_call | solution.py:383

commit v4 on v3

--- a/solution.py
+++ b/solution.py
@@ -186,7 +186,7 @@
         return 0
 
     for half in range(2):
-        lax.fori_loop(0, TILES // 8, functools.partial(column_pass, half), 0, unroll=2)
+        lax.fori_loop(0, TILES // 8, functools.partial(column_pass, half), 0, unroll=4)
         if half == 0:
             to_smem.wait()
             pl.semaphore_wait(sem_round, len(line))
@@ -268,9 +268,9 @@
     for half in range(2):
         sent = sbuf.at[half, pl.ds(1, N - 1)]
         pltpu.make_async_copy(sent, sent, sem_r.at[half]).wait()
-        lax.fori_loop(0, N, functools.partial(widen, half), 0, unroll=8)
-        lax.fori_loop(0, 8, coadd, 0, unroll=4)
-        lax.fori_loop(0, 16, functools.partial(lay, half), 0, unroll=4)
+        lax.fori_loop(0, N, functools.partial(widen, half), 0, unroll=16)
+        lax.fori_loop(0, 8, coadd, 0, unroll=8)
+        lax.fori_loop(0, 16, functools.partial(lay, half), 0, unroll=16)
         for copy in rims[3 * half : 3 + 5 * half]:
             copy.start()
 

time: 53.7 us -> 53.2 us (level)
  no operation moved by 1% of the time
where the time goes in v4:
time: 53.2 us; the launch traced here: 53.1 us
  Pallas kernels  52.5 us (99%)
  between operations  0.64 us (1%)
    pallas_call x1, Pallas kernels, on_device(): pl.pallas_call(kernel, out_shape=(jax.ShapeDtypeStruct((PROWS + 2 * RIM,...  49.3 us
    pallas_call x1, Pallas kernels, on_device(): pl.pallas_call(filter_kernel, out_shape=(jax.ShapeDtypeStruct((PROWS, PCO...  3.13 us

profile of v4, /device:TPU:1, one launch (start us, length us, event | category | flops | bytes accessed | tf_op | source)
XLA Modules:
  0.0 53.1 jit_solution(14618927026070947938)
XLA Ops:
  0.6 49.3 %shard_map.95 = (bf16[160,2304]{1,0:T(8,128)(2,1)}, bf16[128,160]{1,0:T(8,128)(2,1)}, bf16[384,128]{1,0:T(8,128)(2,1)}) custom-call(bf16[1,64,4096]{2,1,0:T(8,128)(2,1)} %exposure.1, s32[1,1,2]{2,1,0:T(1,128)} %offsets_h.1, f32[1,1,2]{2,1,0:T(1,128)} %fraction_h.1, s32[1,64]{1,0:T(1,128)} %patch_h.1, s32[1,64]{1,0:T(1,128)} %slot_h.1, ...), custom_call_target="tpu_custom_call" | custom-call | tf_op jit(solution)/shard_map/pallas_call | solution.py:336
  50.0 3.1 %shard_map.96 = (bf16[128,2048]{1,0:T(8,128)(2,1)}, f32[128,2048]{1,0:T(8,128)}) custom-call(bf16[160,2304]{1,0:T(8,128)(2,1)} %get-tuple-element.5.fr_h, bf16[128,160]{1,0:T(8,128)(2,1)} %get-tuple-element.6.frow_h, bf16[384,128]{1,0:T(8,128)(2,1)} %get-tuple-element.7.fcol_h), custom_call_target="tpu_custom_call" | custom-call | tf_op jit(solution)/shard_map/pallas_call | solution.py:383
